TPU v7x, 512 devices: a whole 4x8x8 slice. The times are simulated.
512 devices in a mesh: dp: 16 (over y_lo, z), seq: 32 (over y_hi, x, core).
Axes of the slice: x: 4, y: 8 (y_hi: 4, y_lo: 2; y = y_hi * 2 + y_lo), z: 8, core: 2. Of those that a mesh axis runs over, the one named last changes fastest.
Arguments:
- queries: bfloat16 [16, 4096, 512], P('dp', 'seq'), may hold values from -6 to 6
- keys: bfloat16 [16, 4096, 512], P('dp', 'seq'), may hold values from -6 to 6
- values: bfloat16 [16, 4096, 512], P('dp', 'seq'), may hold values from -6 to 6
- gates: bfloat16 [16, 4096, 512], P('dp', 'seq'), may hold values from -6 to 6
- out_proj: bfloat16 [512, 1024], replicated, may hold values from -0.25 to 0.25
- out_grad: bfloat16 [16, 4096, 1024], P('dp', 'seq'), may hold values from -6 to 6
- lengths: int32 [16, 4], P('dp'), may hold values from 1 to 2048, 4096 in all within a row
- rel_bias: float32 [4, 16], replicated, may hold values from -2 to 2
Outputs:
- projected: bfloat16 [16, 4096, 1024], P('dp', 'seq')
- query_grad: bfloat16 [16, 4096, 512], P('dp', 'seq')
- key_grad: bfloat16 [16, 4096, 512], P('dp', 'seq')
- value_grad: bfloat16 [16, 4096, 512], P('dp', 'seq')
- bias_grad: float32 [4, 16], replicated
Inputs may be any that keep to these rules, and one draw needn't show every extreme that they name: In every data row the 4 lengths sum to 4096 and the longest is exactly half of 4096.
All inputs are finite; a program needn't handle non-finite values.
Results may differ from a plain program's by a relative error of at most 0.0059.
Values may be sent and summed in bfloat16 or wider, within the bound.
A program may use at most 64 MiB of HBM per device.

v0:
```python
import math
import jax
import jax.numpy as jnp
from jax import lax
from jax.sharding import PartitionSpec as P

epsilon = 1e-05


def positions_and_segments(lengths_row, first_row, row_total):
    ends = jnp.cumsum(lengths_row)
    where_at = first_row + jnp.arange(row_total, dtype=jnp.int32)
    segment = jnp.sum((where_at[:, None] >= ends[None, :]).astype(jnp.int32), axis=1)
    return (where_at, segment)


def segment_bounds(lengths_row, segment_id):
    ends = jnp.cumsum(lengths_row)
    starts = ends - lengths_row
    picked = jnp.arange(lengths_row.shape[0], dtype=jnp.int32) == segment_id
    return (jnp.sum(jnp.where(picked, starts, 0)), jnp.sum(jnp.where(picked, ends, 0)))


def pair_scores(query_block, query_pos, query_seg, key_block, key_pos, key_seg, rel_bias):
    head_width = query_block.shape[2]
    products = jnp.einsum(
        "qhd,khd->hqk", query_block, key_block, preferred_element_type=jnp.float32
    )
    distance = query_pos[:, None] - key_pos[None, :]
    bucket = jnp.zeros(distance.shape, jnp.int32)
    for octave in range(15):
        bucket = bucket + (distance >= 2**octave).astype(jnp.int32)
    one_hot = (bucket[:, :, None] == jnp.arange(rel_bias.shape[1], dtype=jnp.int32)).astype(
        jnp.float32
    )
    shifted = jnp.einsum("hb,qkb->hqk", rel_bias, one_hot, precision=lax.Precision.HIGHEST)
    scores = products * head_width ** (-0.5) + shifted
    allowed = ((query_seg[:, None] == key_seg[None, :]) & (distance >= 0))[None]
    return (scores, allowed, one_hot)


def over_blocks(step_fn, live_fn, running, arrays, first_row):
    row_total = arrays[0].shape[0]
    block_rows = math.gcd(row_total, 512)
    block_count = row_total // block_rows
    stacked = tuple(
        (member.reshape((block_count, block_rows) + member.shape[1:]) for member in arrays)
    )

    def advance(partial_sum, element):
        block_index, pieces = element
        block_first = first_row + block_index * block_rows
        updated = lax.cond(
            live_fn(block_first, block_rows),
            lambda state: step_fn(state, pieces, block_first),
            lambda state: state,
            partial_sum,
        )
        return (updated, None)

    result, unused = lax.scan(advance, running, (jnp.arange(block_count, dtype=jnp.int32), stacked))
    return result


def shards(queries, keys, values, gates, out_proj, out_grad, lengths, rel_bias):
    heads = rel_bias.shape[0]
    tok_rows = queries.shape[1]
    feature_width = queries.shape[2]
    head_width = feature_width // heads
    own_queries = queries[0].reshape(tok_rows, heads, head_width)
    own_keys = keys[0].reshape(tok_rows, heads, head_width)
    own_values = values[0].reshape(tok_rows, heads, head_width)
    own_gates = gates[0].reshape(tok_rows, heads, head_width)
    lengths_row = lengths[0]
    own_first = lax.axis_index("seq") * tok_rows
    own_last = own_first + tok_rows - 1
    own_pos, own_seg = positions_and_segments(lengths_row, own_first, tok_rows)
    earliest_start, unused_end = segment_bounds(lengths_row, own_seg[0])
    unused_start, latest_end = segment_bounds(lengths_row, own_seg[tok_rows - 1])
    zero_heads = jnp.zeros((tok_rows, heads, head_width), jnp.float32)

    def keys_live(block_first, count):
        return (block_first <= own_last) & (block_first + count > earliest_start)

    def queries_live(block_first, count):
        return (block_first + count > own_first) & (block_first < latest_end)

    def forward_step(running, pieces, first_row):
        key_block, value_block = pieces
        key_pos, key_seg = positions_and_segments(lengths_row, first_row, key_block.shape[0])
        scores, allowed, one_hot = pair_scores(
            own_queries, own_pos, own_seg, key_block, key_pos, key_seg, rel_bias
        )
        weights = jnp.where(allowed, jax.nn.silu(scores), 0.0).astype(jnp.bfloat16)
        return running + jnp.einsum(
            "hqk,khd->qhd", weights, value_block, preferred_element_type=jnp.float32
        )

    all_keys, all_values = (
        lax.all_gather(own_keys, "seq", axis=0, tiled=True),
        lax.all_gather(own_values, "seq", axis=0, tiled=True),
    )
    mixed = over_blocks(forward_step, keys_live, zero_heads, (all_keys, all_values), 0)
    average = jnp.mean(mixed, axis=2, keepdims=True)
    centred = mixed - average
    variance = jnp.mean(centred * centred, axis=2, keepdims=True)
    inverse = lax.rsqrt(variance + epsilon)
    normed = centred * inverse
    gated = (
        (normed * own_gates.astype(jnp.float32))
        .astype(jnp.bfloat16)
        .reshape(tok_rows, feature_width)
    )
    projected = jnp.dot(gated, out_proj, preferred_element_type=jnp.float32).astype(jnp.bfloat16)
    gated_grad = jnp.einsum("te,ce->tc", out_grad[0], out_proj, preferred_element_type=jnp.float32)
    normed_grad = gated_grad.reshape(tok_rows, heads, head_width) * own_gates.astype(jnp.float32)
    mixed_grad = (
        normed_grad
        - jnp.mean(normed_grad, axis=2, keepdims=True)
        - normed * jnp.mean(normed_grad * normed, axis=2, keepdims=True)
    ) * inverse
    mixed_grad = mixed_grad.astype(jnp.bfloat16)

    def query_step(running, pieces, first_row):
        key_block, value_block = pieces
        key_pos, key_seg = positions_and_segments(lengths_row, first_row, key_block.shape[0])
        scores, allowed, one_hot = pair_scores(
            own_queries, own_pos, own_seg, key_block, key_pos, key_seg, rel_bias
        )
        sigmoid_s = jax.nn.sigmoid(scores)
        attn_grad = jnp.einsum(
            "qhd,khd->hqk", mixed_grad, value_block, preferred_element_type=jnp.float32
        )
        score_grad = jnp.where(
            allowed, attn_grad * sigmoid_s * (1.0 + scores * (1.0 - sigmoid_s)), 0.0
        )
        score_low = score_grad.astype(jnp.bfloat16)
        return running + jnp.einsum(
            "hqk,khd->qhd", score_low, key_block, preferred_element_type=jnp.float32
        )

    def key_step(running, pieces, first_row):
        key_total, value_total, bias_part = running
        query_block, grad_block = pieces
        query_pos, query_seg = positions_and_segments(lengths_row, first_row, query_block.shape[0])
        scores, allowed, one_hot = pair_scores(
            query_block, query_pos, query_seg, own_keys, own_pos, own_seg, rel_bias
        )
        sigmoid_s = jax.nn.sigmoid(scores)
        weights = jnp.where(allowed, scores * sigmoid_s, 0.0).astype(jnp.bfloat16)
        attn_grad = jnp.einsum(
            "qhd,khd->hqk", grad_block, own_values, preferred_element_type=jnp.float32
        )
        score_grad = jnp.where(
            allowed, attn_grad * sigmoid_s * (1.0 + scores * (1.0 - sigmoid_s)), 0.0
        )
        score_low = score_grad.astype(jnp.bfloat16)
        key_total = key_total + jnp.einsum(
            "hqk,qhd->khd", score_low, query_block, preferred_element_type=jnp.float32
        )
        value_total = value_total + jnp.einsum(
            "hqk,qhd->khd", weights, grad_block, preferred_element_type=jnp.float32
        )
        bias_terms = jnp.einsum("hqk,qkb->hb", score_grad, one_hot, precision=lax.Precision.HIGHEST)
        return (key_total, value_total, bias_part + bias_terms)

    first_row = jnp.int32(0)
    query_total = zero_heads
    key_total = zero_heads
    value_total = zero_heads
    bias_part = jnp.zeros(rel_bias.shape, jnp.float32)
    query_piece = lax.all_gather(own_queries, "seq", axis=0, tiled=True)
    grad_piece = lax.all_gather(mixed_grad, "seq", axis=0, tiled=True)
    key_piece = lax.all_gather(own_keys, "seq", axis=0, tiled=True)
    value_piece = lax.all_gather(own_values, "seq", axis=0, tiled=True)
    query_total = over_blocks(
        query_step, keys_live, query_total, (key_piece, value_piece), first_row
    )
    key_total, value_total, bias_part = over_blocks(
        key_step,
        queries_live,
        (key_total, value_total, bias_part),
        (query_piece, grad_piece),
        first_row,
    )
    query_total, key_total, value_total, bias_part = (
        query_total,
        key_total,
        value_total,
        bias_part,
    )
    bias_grad = lax.psum(bias_part, ("dp", "seq"))
    query_grad = query_total.reshape(1, tok_rows, feature_width).astype(jnp.bfloat16)
    key_grad = key_total.reshape(1, tok_rows, feature_width).astype(jnp.bfloat16)
    value_grad = value_total.reshape(1, tok_rows, feature_width).astype(jnp.bfloat16)
    return (projected[None], query_grad, key_grad, value_grad, bias_grad)


def solution(mesh):
    in_specs = (
        P("dp", "seq", None),
        P("dp", "seq", None),
        P("dp", "seq", None),
        P("dp", "seq", None),
        P(),
        P("dp", "seq", None),
        P("dp", None),
        P(),
    )
    out_specs = (
        P("dp", "seq", None),
        P("dp", "seq", None),
        P("dp", "seq", None),
        P("dp", "seq", None),
        P(),
    )
    return jax.shard_map(shards, mesh=mesh, in_specs=in_specs, out_specs=out_specs, check_vma=False)
```

profile of v0, /device:TPU:1, one launch (start us, length us, event | category | flops | bytes accessed | tf_op | source)
XLA Modules:
  0.0 500.8 jit_solution(6191673273034674706)
XLA Ops:
  19.5 68.8 %all-gather.5.cloned.1.call-done = bf16[4096,4,128]{0,2,1:T(8,128)(2,1)} async-done(((bf16[128,4,128]{0,2,1:T(8,128)(2,1)}), bf16[4096,4,128]{0,2,1:T(8,128)(2,1)}) %all-gather.5.cloned.1.call-update) | async-done | bytes 4194320 | tf_op jit(solution)/shard_map/all_gather | solution.py:100
  88.3 6.4 %copy.103 = bf16[64,8,8,512]{3,2,1,0:T(8,128)(2,1)} copy(bf16[64,8,8,512]{3,1,2,0:T(8,128)(2,1)} %bitcast.164) | data formatting | bytes 8388608
  94.6 7.9 %copy.82 = bf16[8,512,4,128]{3,1,2,0:T(8,128)(2,1)} copy(bf16[8,512,4,128]{1,0,3,2:T(8,128)(2,1)} %bitcast.159) | data formatting | bytes 8388608
  102.6 58.8 %all-gather.7.cloned.1.call-done = bf16[4096,4,128]{0,2,1:T(8,128)(2,1)} async-done(((bf16[128,4,128]{0,2,1:T(8,128)(2,1)}), bf16[4096,4,128]{0,2,1:T(8,128)(2,1)}) %all-gather.7.cloned.1.call-update) | async-done | bytes 4194320 | tf_op jit(solution)/shard_map/all_gather | solution.py:101
  161.3 6.4 %copy.104 = bf16[64,8,8,512]{3,2,1,0:T(8,128)(2,1)} copy(bf16[64,8,8,512]{3,1,2,0:T(8,128)(2,1)} %bitcast.165) | data formatting | bytes 8388608
  167.7 7.9 %copy.84 = bf16[8,512,4,128]{3,1,2,0:T(8,128)(2,1)} copy(bf16[8,512,4,128]{1,0,3,2:T(8,128)(2,1)} %bitcast.160) | data formatting | bytes 8388608
  176.2 25.5 %while.44 = (s32[]{:T(128)}, f32[128,4,128]{2,0,1:T(8,128)S(1)}, s32[8]{0:T(128)}, s32[]{:T(128)}, s32[]{:T(128)}, /*index=5*/s32[128]{0:T(128)S(1)}, s32[4]{0:T...) while((s32[]{:T(128)}, f32[128,4,128]{2,0,1:T(8,128)S(1)}, ...), condition=%wide.region_8.9_spmd.clone, body=%wide.region_3.8_spmd.clone.sunk | while | flops 190978192 | bytes 7094895 | solution.py:61
  178.7 5.4 %conditional.10 = (f32[128,4,128]{2,0,1:T(8,128)S(1)}) conditional(s32[]{:T(128)} %convert_element_type.601, f32[128,4,128]{2,0,1:T(8,128)S(1)} %get-tuple-element.1113, (s32[128]{0:T(128)S(1)}, s32[]{:T(128)}, s32[4]{0:T(128)}, s32[]{:T(128)}, bf16[8,512,4,128]{3,1,2,0:T(8,128)(2,1)}, /*index=5*/s32[]{:T(128)}, bf16[128,4,128]{2,0,1:T(8,128)(2,1)S(1)}, ...), branch_computations={%region_4.4_spmd, %region_5.7_spmd} | conditional | flops 190978192 | bytes 7094084 | solution.py:53
  209.1 27.4 %while.45 = (s32[]{:T(128)}, f32[128,4,128]{2,0,1:T(8,128)}, s32[8]{0:T(128)}, s32[]{:T(128)}, s32[]{:T(128)}, /*index=5*/s32[128]{0:T(128)S(1)}, s32[4]{0:T(128...) while((s32[]{:T(128)}, f32[128,4,128]{2,0,1:T(8,128)}, ...), condition=%wide.region_18.19_spmd.clone, body=%wide.region_13.18_spmd.clone.sunk | while | flops 259135632 | bytes 9847935 | solution.py:61
  211.6 7.6 %conditional.11 = (f32[128,4,128]{2,0,1:T(8,128)}) conditional(s32[]{:T(128)} %convert_element_type.602, f32[128,4,128]{2,0,1:T(8,128)} %get-tuple-element.1159, (s32[128]{0:T(128)S(1)}, s32[]{:T(128)}, s32[4]{0:T(128)}, s32[]{:T(128)}, bf16[8,512,4,128]{3,1,2,0:T(8,128)(2,1)}, /*index=5*/s32[]{:T(128)}, bf16[128,4,128]{2,0,1:T(8,128)(2,1)}, ...), branch_computations={%region_14.14_spmd, %region_15.17_spmd} | conditional | flops 259135632 | bytes 9847108 | solution.py:53
  238.4 6.3 %copy.92 = bf16[4096,4,128]{2,0,1:T(8,128)(2,1)} copy(bf16[4096,4,128]{0,2,1:T(8,128)(2,1)} %all-gather.11.cloned.1.call-done) | data formatting | bytes 8388608 | tf_op jit(solution)/shard_map/all_gather | solution.py:172
  244.7 4.6 copy.95
  250.3 56.5 %all-gather.9.cloned.1.call-done = bf16[4096,4,128]{0,2,1:T(8,128)(2,1)} async-done(((bf16[128,4,128]{0,2,1:T(8,128)(2,1)}), bf16[4096,4,128]{0,2,1:T(8,128)(2,1)}) %all-gather.9.cloned.1.call-update) | async-done | bytes 4194320 | tf_op jit(solution)/shard_map/all_gather | solution.py:173
  306.8 6.4 %copy.105 = bf16[64,8,8,512]{3,2,1,0:T(8,128)(2,1)} copy(bf16[64,8,8,512]{3,1,2,0:T(8,128)(2,1)} %bitcast.163) | data formatting | bytes 8388608
  313.2 8.0 %copy.93 = bf16[8,512,4,128]{3,1,2,0:T(8,128)(2,1)} copy(bf16[8,512,4,128]{1,0,3,2:T(8,128)(2,1)} %bitcast.162) | data formatting | bytes 8388608
  321.2 64.0 %while.46 = (s32[]{:T(128)}, f32[128,4,128]{2,0,1:T(8,128)S(1)}, f32[128,4,128]{2,0,1:T(8,128)S(1)}, f32[4,16]{1,0:T(4,128)S(1)}, s32[8]{0:T(128)S(1)}, /*index=...) while((s32[]{:T(128)}, f32[128,4,128]{2,0,1:T(8,128)S(1)}, ...), condition=%wide.region_25.26_spmd.clone.clone, body=%wide.region_20.25_spmd.clone.clone.sunk | while | flops 379263168 | bytes 17516744 | solution.py:61
  323.1 12.2 %conditional.12 = ((f32[128,4,128]{2,0,1:T(8,128)S(1)}, f32[128,4,128]{2,0,1:T(8,128)S(1)}, f32[4,16]{1,0:T(4,128)S(1)})) conditional(s32[]{:T(128)} %convert_element_type.603, (f32[128,4,128]{2,0,1:T(8,128)S(1)}, f32[128,4,128]{2,0,1:T(8,128)S(1)}, f32[4,16]{1,0:T(4,128)S(1)}) %tuple.118, (s32[]{:T(128)}, s32[4]{0:T(128)S(1)}, s32[128]{0:T(128)S(1)}, ...), branch_computations={%region_21.21_spmd, %region_22.24_spmd} | conditional | flops 379263168 | bytes 17515868 | solution.py:53
  332.4 2.9 fusion.74
  337.2 12.2 %conditional.12 = ((f32[128,4,128]{2,0,1:T(8,128)S(1)}, f32[128,4,128]{2,0,1:T(8,128)S(1)}, f32[4,16]{1,0:T(4,128)S(1)})) conditional(s32[]{:T(128)} %convert_element_type.603, (f32[128,4,128]{2,0,1:T(8,128)S(1)}, f32[128,4,128]{2,0,1:T(8,128)S(1)}, f32[4,16]{1,0:T(4,128)S(1)}) %tuple.118, (s32[]{:T(128)}, s32[4]{0:T(128)S(1)}, s32[128]{0:T(128)S(1)}, ...), branch_computations={%region_21.21_spmd, %region_22.24_spmd} | conditional | flops 379263168 | bytes 17515868 | solution.py:53
  346.5 2.9 fusion.74
  351.3 12.2 %conditional.12 = ((f32[128,4,128]{2,0,1:T(8,128)S(1)}, f32[128,4,128]{2,0,1:T(8,128)S(1)}, f32[4,16]{1,0:T(4,128)S(1)})) conditional(s32[]{:T(128)} %convert_element_type.603, (f32[128,4,128]{2,0,1:T(8,128)S(1)}, f32[128,4,128]{2,0,1:T(8,128)S(1)}, f32[4,16]{1,0:T(4,128)S(1)}) %tuple.118, (s32[]{:T(128)}, s32[4]{0:T(128)S(1)}, s32[128]{0:T(128)S(1)}, ...), branch_computations={%region_21.21_spmd, %region_22.24_spmd} | conditional | flops 379263168 | bytes 17515868 | solution.py:53
  360.6 2.9 fusion.74
  365.4 12.2 %conditional.12 = ((f32[128,4,128]{2,0,1:T(8,128)S(1)}, f32[128,4,128]{2,0,1:T(8,128)S(1)}, f32[4,16]{1,0:T(4,128)S(1)})) conditional(s32[]{:T(128)} %convert_element_type.603, (f32[128,4,128]{2,0,1:T(8,128)S(1)}, f32[128,4,128]{2,0,1:T(8,128)S(1)}, f32[4,16]{1,0:T(4,128)S(1)}) %tuple.118, (s32[]{:T(128)}, s32[4]{0:T(128)S(1)}, s32[128]{0:T(128)S(1)}, ...), branch_computations={%region_21.21_spmd, %region_22.24_spmd} | conditional | flops 379263168 | bytes 17515868 | solution.py:53
  387.0 107.3 %psum.7 = f32[4,16]{1,0:T(4,128)} all-reduce(f32[4,16]{1,0:T(4,128)S(1)} %get-tuple-element.505), channel_id=1, replica_groups=mesh['dp'=16,'seq'=32] {'dp','seq'}, use_global_device_ids=true, to_apply=%region_26.27 | all-reduce | flops 64 | bytes 512 | tf_op jit(solution)/shard_map/psum | solution.py:192
  (206 shorter events, 102.6 us)
Async XLA Ops:
  7.2 194.9 %copy-start = (bf16[512,1024]{1,0:T(8,128)(2,1)S(1)}, bf16[512,1024]{1,0:T(8,128)(2,1)}, u32[]{:S(2)}) copy-start(bf16[512,1024]{1,0:T(8,128)(2,1)} %param.24) | copy-start | bytes 3145732
  7.2 81.1 %all-gather.5.cloned.1.call-start = ((), (), s32[]{:S(2)}) async-start(), calls=%async_computation | async-start | bytes 4325376 | tf_op jit(solution)/shard_map/all_gather | solution.py:100
  9.0 152.3 %all-gather.7.cloned.1.call-start = ((), (), s32[]{:S(2)}) async-start(), calls=%async_computation.1 | async-start | bytes 4325376 | tf_op jit(solution)/shard_map/all_gather | solution.py:101
  10.7 227.6 %all-gather.11.cloned.1.call-start = ((), (), s32[]{:S(2)}) async-start(), calls=%async_computation.3 | async-start | bytes 4325376 | tf_op jit(solution)/shard_map/all_gather | solution.py:172
  12.5 294.3 %all-gather.9.cloned.1.call-start = ((), (), s32[]{:S(2)}) async-start(), calls=%async_computation.2 | async-start | bytes 4325376 | tf_op jit(solution)/shard_map/all_gather | solution.py:173
  167.7 8.5 %copy-start.4 = (f32[4,16]{1,0:T(4,128)S(1)}, f32[4,16]{1,0:T(4,128)}, u32[]{:S(2)}) copy-start(f32[4,16]{1,0:T(4,128)} %param.27) | copy-start | bytes 772
  201.7 3.6 copy-start.3
  201.7 4.4 copy-start.2
  313.2 8.0 %copy-start.5 = (bf16[128,4,128]{2,0,1:T(8,128)(2,1)S(1)}, bf16[128,4,128]{2,0,1:T(8,128)(2,1)}, u32[]{:S(2)}) copy-start(bf16[128,4,128]{2,0,1:T(8,128)(2,1)} %copy.94) | copy-start | bytes 393220
  313.2 8.0 %copy-start.6 = (s32[4]{0:T(128)S(1)}, s32[4]{0:T(128)}, u32[]{:S(2)}) copy-start(s32[4]{0:T(128)} %get-tuple-element.1271) | copy-start | bytes 52
  385.2 109.0 %copy-start.1 = (bf16[512,1024]{1,0:T(8,128)(2,1)S(1)}, bf16[512,1024]{1,0:T(8,128)(2,1)}, u32[]{:S(2)}) copy-start(bf16[512,1024]{1,0:T(8,128)(2,1)} %param.24) | copy-start | bytes 3145732
Sparse Core Ops, SparseCore 0:
  11.6 76.5 all-gather.4
  91.9 69.3 all-gather.6
  165.0 69.4 all-gather.10
  237.3 69.4 all-gather.8
where the time goes:
time: 504 us; the launch traced here: 501 us
  waiting for transfers between devices  184 us (37%)
  blocking collectives  107 us (21%)
  local copies, waits for them, and re-layouts  99.6 us (20%)
  matrix products  51.6 us (10%)
  loops' own time  30.7 us (6%)
  between operations  14 us (3%)
  other arithmetic  13.4 us (3%)
    psum x1, blocking collectives, shards(): bias_grad = lax.psum(bias_part, ('dp', 'seq'))  107 us
    all_gather x1, waiting for transfers between devices, shards(): lax.all_gather(own_keys, 'seq', axis=0, tiled=True)  68.8 us
    all_gather x1, waiting for transfers between devices, shards(): lax.all_gather(own_values, 'seq', axis=0, tiled=True)  58.8 us
    all_gather x1, waiting for transfers between devices, shards(): grad_piece = lax.all_gather(mixed_grad, 'seq', axis=0, tiled=True)  56.5 us
    unnamed x28, local copies, waits for them, and re-layouts  56.2 us
    another operation x3, loops' own time, over_blocks(): lax.scan(advance, running, (jnp.arange(block_count, dtype=jnp.int32), sta...  29.9 us
    dynamic_slice x24, local copies, waits for them, and re-layouts, over_blocks(): lax.scan(advance, running, (jnp.arange(block_count, dtype=jnp.int32), sta...  24.9 us
    dot_general x4, matrix products, key_step(): jnp.einsum('hqk,qkb->hb', score_grad, one_hot, precision=lax.Precision.HI...  11.5 us
  transfers between devices with their start and end apart: 4, of which 3 were waited for; matrix products, arithmetic and copies ran while one was open for 19% of the time, Pallas kernels for 0%

commit v1 on v0

--- a/solution.py
+++ b/solution.py
@@ -5,6 +5,17 @@
 from jax.sharding import PartitionSpec as P
 
 epsilon = 1e-05
+
+
+def render_regions(shard_in, page, axis_id):
+    then = jnp.split(
+        jax.lax.all_gather(
+            jnp.concatenate([shard_in, page], 1), axis_name=axis_id, axis=0, tiled=True
+        ),
+        [shard_in.shape[1]],
+        axis=1,
+    )
+    return then
 
 
 def positions_and_segments(lengths_row, first_row, row_total):
@@ -170,8 +181,7 @@
     value_total = zero_heads
     bias_part = jnp.zeros(rel_bias.shape, jnp.float32)
     query_piece = lax.all_gather(own_queries, "seq", axis=0, tiled=True)
-    grad_piece = lax.all_gather(mixed_grad, "seq", axis=0, tiled=True)
-    key_piece = lax.all_gather(own_keys, "seq", axis=0, tiled=True)
+    grad_piece, key_piece = render_regions(mixed_grad, own_keys, axis_id="seq")
     value_piece = lax.all_gather(own_values, "seq", axis=0, tiled=True)
     query_total = over_blocks(
         query_step, keys_live, query_total, (key_piece, value_piece), first_row

time: 504 us -> 609 us (1.21)
  the two profiles are of different devices: /device:TPU:1 before, /device:TPU:56 now
where the time goes in v1:
time: 609 us; the launch traced here: 607 us
  waiting for transfers between devices  212 us (35%)
  blocking collectives  145 us (24%)
  local copies, waits for them, and re-layouts  115 us (19%)
  matrix products  65.7 us (11%)
  loops' own time  33.4 us (5%)
  other arithmetic  20.7 us (3%)
  between operations  14 us (2%)
    psum x1, blocking collectives, shards(): bias_grad = lax.psum(bias_part, ('dp', 'seq'))  145 us
    all_gather x1, waiting for transfers between devices, render_regions(): jax.lax.all_gather(jnp.concatenate([shard_in, page], 1), axis_name=axis_i...  79.7 us
    unnamed x30, local copies, waits for them, and re-layouts  68.5 us
    all_gather x1, waiting for transfers between devices, shards(): lax.all_gather(own_keys, 'seq', axis=0, tiled=True)  63.9 us
    all_gather x1, waiting for transfers between devices, shards(): lax.all_gather(own_values, 'seq', axis=0, tiled=True)  58.8 us
    another operation x3, loops' own time, over_blocks(): lax.scan(advance, running, (jnp.arange(block_count, dtype=jnp.int32), sta...  32.5 us
    dynamic_slice x24, local copies, waits for them, and re-layouts, over_blocks(): lax.scan(advance, running, (jnp.arange(block_count, dtype=jnp.int32), sta...  19 us
    dot_general x12, matrix products, pair_scores(): jnp.einsum('hb,qkb->hqk', rel_bias, one_hot, precision=lax.Precision.HIGH...  15.3 us
  transfers between devices with their start and end apart: 4, of which 4 were waited for; matrix products, arithmetic and copies ran while one was open for 15% of the time, Pallas kernels for 0%

profile of v1, /device:TPU:56, one launch (start us, length us, event | category | flops | bytes accessed | tf_op | source)
XLA Modules:
  0.0 606.8 jit_solution(16409471446394818694)
XLA Ops:
  19.4 63.9 %all-gather.5.cloned.1.call-done = bf16[4096,4,128]{0,2,1:T(8,128)(2,1)} async-done(((bf16[128,4,128]{0,2,1:T(8,128)(2,1)}), bf16[4096,4,128]{0,2,1:T(8,128)(2,1)}) %all-gather.5.cloned.1.call-update) | async-done | bytes 4194320 | tf_op jit(solution)/shard_map/all_gather | solution.py:111
  83.2 6.4 %copy.105 = bf16[64,8,8,512]{3,2,1,0:T(8,128)(2,1)} copy(bf16[64,8,8,512]{3,1,2,0:T(8,128)(2,1)} %bitcast.172) | data formatting | bytes 8388608
  89.6 7.9 %copy.84 = bf16[8,512,4,128]{3,1,2,0:T(8,128)(2,1)} copy(bf16[8,512,4,128]{1,0,3,2:T(8,128)(2,1)} %bitcast.165) | data formatting | bytes 8388608
  97.5 58.8 %all-gather.7.cloned.1.call-done = bf16[4096,4,128]{0,2,1:T(8,128)(2,1)} async-done(((bf16[128,4,128]{0,2,1:T(8,128)(2,1)}), bf16[4096,4,128]{0,2,1:T(8,128)(2,1)}) %all-gather.7.cloned.1.call-update) | async-done | bytes 4194320 | tf_op jit(solution)/shard_map/all_gather | solution.py:112
  156.3 6.3 %copy.106 = bf16[64,8,8,512]{3,2,1,0:T(8,128)(2,1)} copy(bf16[64,8,8,512]{3,1,2,0:T(8,128)(2,1)} %bitcast.173) | data formatting | bytes 8388608
  162.6 7.9 %copy.86 = bf16[8,512,4,128]{3,1,2,0:T(8,128)(2,1)} copy(bf16[8,512,4,128]{1,0,3,2:T(8,128)(2,1)} %bitcast.166) | data formatting | bytes 8388608
  170.6 42.8 %while.44 = (s32[]{:T(128)}, f32[128,4,128]{2,0,1:T(8,128)S(1)}, s32[8]{0:T(128)S(1)}, s32[]{:T(128)}, s32[]{:T(128)}, /*index=5*/s32[128]{0:T(128)S(1)}, s32[4]...) while((s32[]{:T(128)}, f32[128,4,128]{2,0,1:T(8,128)S(1)}, ...), condition=%wide.region_8.9_spmd.clone, body=%wide.region_3.8_spmd.clone.sunk | while | flops 190978192 | bytes 7094887 | solution.py:72
  183.9 5.4 conditional.10
  219.5 9.8 %all-gather.11.cloned.1.call-done = bf16[4096,4,128]{0,2,1:T(8,128)(2,1)} async-done(((bf16[128,4,128]{0,2,1:T(8,128)(2,1)}), bf16[4096,4,128]{0,2,1:T(8,128)(2,1)}) %all-gather.11.cloned.1.call-update) | async-done | bytes 4194320 | tf_op jit(solution)/shard_map/all_gather | solution.py:183
  229.3 6.3 %copy.94 = bf16[4096,4,128]{2,0,1:T(8,128)(2,1)} copy(bf16[4096,4,128]{0,2,1:T(8,128)(2,1)} %all-gather.11.cloned.1.call-done) | data formatting | bytes 8388608 | tf_op jit(solution)/shard_map/all_gather | solution.py:183
  241.2 79.7 %all-gather.9.cloned.1.call-done = bf16[4096,8,128]{0,2,1:T(8,128)(2,1)} async-done(((bf16[128,8,128]{0,2,1:T(8,128)(2,1)}), bf16[4096,8,128]{0,2,1:T(8,128)(2,1)}) %all-gather.9.cloned.1.call-update) | async-done | bytes 8388624 | tf_op jit(solution)/shard_map/all_gather | solution.py:12
  330.3 7.9 %copy.95 = bf16[8,512,4,128]{3,1,2,0:T(8,128)(2,1)} copy(bf16[8,512,4,128]{1,0,3,2:T(8,128)(2,1)} %bitcast.168) | data formatting | bytes 8388608
  339.5 50.3 %while.46 = (s32[]{:T(128)}, f32[128,4,128]{2,0,1:T(8,128)S(1)}, f32[128,4,128]{2,0,1:T(8,128)}, f32[4,16]{1,0:T(4,128)S(1)}, s32[8]{0:T(128)}, /*index=5*/s32[]...) while((s32[]{:T(128)}, f32[128,4,128]{2,0,1:T(8,128)S(1)}, ...), condition=%wide.region_25.26_spmd.clone.clone, body=%wide.region_20.25_spmd.clone.clone.sunk | while | flops 379263168 | bytes 19876116 | solution.py:72
  357.2 15.0 %conditional.12 = ((f32[128,4,128]{2,0,1:T(8,128)S(1)}, f32[128,4,128]{2,0,1:T(8,128)}, f32[4,16]{1,0:T(4,128)S(1)})) conditional(s32[]{:T(128)} %convert_element_type.603, (f32[128,4,128]{2,0,1:T(8,128)S(1)}, f32[128,4,128]{2,0,1:T(8,128)}, f32[4,16]{1,0:T(4,128)S(1)}) %tuple.119, (s32[]{:T(128)}, s32[4]{0:T(128)S(1)}, s32[128]{0:T(128)S(1)}, ...), branch_computations={%region_21.21_spmd, %region_22.24_spmd} | conditional | flops 379263168 | bytes 19875248 | solution.py:64
  374.7 15.0 %conditional.12 = ((f32[128,4,128]{2,0,1:T(8,128)S(1)}, f32[128,4,128]{2,0,1:T(8,128)}, f32[4,16]{1,0:T(4,128)S(1)})) conditional(s32[]{:T(128)} %convert_element_type.603, (f32[128,4,128]{2,0,1:T(8,128)S(1)}, f32[128,4,128]{2,0,1:T(8,128)}, f32[4,16]{1,0:T(4,128)S(1)}) %tuple.119, (s32[]{:T(128)}, s32[4]{0:T(128)S(1)}, s32[128]{0:T(128)S(1)}, ...), branch_computations={%region_21.21_spmd, %region_22.24_spmd} | conditional | flops 379263168 | bytes 19875248 | solution.py:64
  392.4 145.2 %psum.7 = f32[4,16]{1,0:T(4,128)} all-reduce(f32[4,16]{1,0:T(4,128)S(1)} %get-tuple-element.505), channel_id=1, replica_groups=mesh['dp'=16,'seq'=32] {'dp','seq'}, use_global_device_ids=true, to_apply=%region_26.27 | all-reduce | flops 64 | bytes 512 | tf_op jit(solution)/shard_map/psum | solution.py:202
  537.6 6.4 %copy.107 = bf16[64,8,8,512]{3,2,1,0:T(8,128)(2,1)} copy(bf16[64,8,8,512]{3,1,2,0:T(8,128)(2,1)} %bitcast.170) | data formatting | bytes 8388608
  544.0 8.0 %copy.91 = bf16[8,512,4,128]{3,1,2,0:T(8,128)(2,1)} copy(bf16[8,512,4,128]{1,0,3,2:T(8,128)(2,1)} %bitcast.169) | data formatting | bytes 8388608
  552.0 47.0 %while.45 = (s32[]{:T(128)}, f32[128,4,128]{2,0,1:T(8,128)S(1)}, s32[8]{0:T(128)S(1)}, s32[]{:T(128)}, s32[]{:T(128)}, /*index=5*/s32[128]{0:T(128)S(1)}, s32[4]...) while((s32[]{:T(128)}, f32[128,4,128]{2,0,1:T(8,128)S(1)}, ...), condition=%wide.region_18.19_spmd.clone, body=%wide.region_13.18_spmd.clone.sunk | while | flops 259135632 | bytes 9847927 | solution.py:72
  558.0 6.2 %conditional.11 = (f32[128,4,128]{2,0,1:T(8,128)S(1)}) conditional(s32[]{:T(128)} %convert_element_type.602, f32[128,4,128]{2,0,1:T(8,128)S(1)} %get-tuple-element.1161, (s32[128]{0:T(128)S(1)}, s32[]{:T(128)}, s32[4]{0:T(128)S(1)}, s32[]{:T(128)}, bf16[8,512,4,128]{3,1,2,0:T(8,128)(2,1)}, /*index=5*/s32[]{:T(128)}, ...), branch_computations={%region_14.14_spmd, %region_15.17_spmd} | conditional | flops 259135632 | bytes 9847108 | solution.py:64
  566.2 6.2 %conditional.11 = (f32[128,4,128]{2,0,1:T(8,128)S(1)}) conditional(s32[]{:T(128)} %convert_element_type.602, f32[128,4,128]{2,0,1:T(8,128)S(1)} %get-tuple-element.1161, (s32[128]{0:T(128)S(1)}, s32[]{:T(128)}, s32[4]{0:T(128)S(1)}, s32[]{:T(128)}, bf16[8,512,4,128]{3,1,2,0:T(8,128)(2,1)}, /*index=5*/s32[]{:T(128)}, ...), branch_computations={%region_14.14_spmd, %region_15.17_spmd} | conditional | flops 259135632 | bytes 9847108 | solution.py:64
  574.4 6.2 %conditional.11 = (f32[128,4,128]{2,0,1:T(8,128)S(1)}) conditional(s32[]{:T(128)} %convert_element_type.602, f32[128,4,128]{2,0,1:T(8,128)S(1)} %get-tuple-element.1161, (s32[128]{0:T(128)S(1)}, s32[]{:T(128)}, s32[4]{0:T(128)S(1)}, s32[]{:T(128)}, bf16[8,512,4,128]{3,1,2,0:T(8,128)(2,1)}, /*index=5*/s32[]{:T(128)}, ...), branch_computations={%region_14.14_spmd, %region_15.17_spmd} | conditional | flops 259135632 | bytes 9847108 | solution.py:64
  582.6 6.2 %conditional.11 = (f32[128,4,128]{2,0,1:T(8,128)S(1)}) conditional(s32[]{:T(128)} %convert_element_type.602, f32[128,4,128]{2,0,1:T(8,128)S(1)} %get-tuple-element.1161, (s32[128]{0:T(128)S(1)}, s32[]{:T(128)}, s32[4]{0:T(128)S(1)}, s32[]{:T(128)}, bf16[8,512,4,128]{3,1,2,0:T(8,128)(2,1)}, /*index=5*/s32[]{:T(128)}, ...), branch_computations={%region_14.14_spmd, %region_15.17_spmd} | conditional | flops 259135632 | bytes 9847108 | solution.py:64
  590.8 6.2 %conditional.11 = (f32[128,4,128]{2,0,1:T(8,128)S(1)}) conditional(s32[]{:T(128)} %convert_element_type.602, f32[128,4,128]{2,0,1:T(8,128)S(1)} %get-tuple-element.1161, (s32[128]{0:T(128)S(1)}, s32[]{:T(128)}, s32[4]{0:T(128)S(1)}, s32[]{:T(128)}, bf16[8,512,4,128]{3,1,2,0:T(8,128)(2,1)}, /*index=5*/s32[]{:T(128)}, ...), branch_computations={%region_14.14_spmd, %region_15.17_spmd} | conditional | flops 259135632 | bytes 9847108 | solution.py:64
  (276 shorter events, 166.8 us)
Async XLA Ops:
  7.2 206.7 %copy-start = (bf16[512,1024]{1,0:T(8,128)(2,1)S(1)}, bf16[512,1024]{1,0:T(8,128)(2,1)}, u32[]{:S(2)}) copy-start(bf16[512,1024]{1,0:T(8,128)(2,1)} %param.24) | copy-start | bytes 3145732
  7.2 76.0 %all-gather.5.cloned.1.call-start = ((), (), s32[]{:S(2)}) async-start(), calls=%async_computation | async-start | bytes 4325376 | tf_op jit(solution)/shard_map/all_gather | solution.py:111
  9.0 147.3 %all-gather.7.cloned.1.call-start = ((), (), s32[]{:S(2)}) async-start(), calls=%async_computation.1 | async-start | bytes 4325376 | tf_op jit(solution)/shard_map/all_gather | solution.py:112
  10.7 218.6 %all-gather.11.cloned.1.call-start = ((), (), s32[]{:S(2)}) async-start(), calls=%async_computation.3 | async-start | bytes 4325376 | tf_op jit(solution)/shard_map/all_gather | solution.py:183
  12.5 308.5 %all-gather.9.cloned.1.call-start = ((), (), s32[]{:S(2)}) async-start(), calls=%async_computation.2 | async-start | bytes 8650752 | tf_op jit(solution)/shard_map/all_gather | solution.py:12
  162.6 8.0 %copy-start.7 = (f32[4,16]{1,0:T(4,128)S(1)}, f32[4,16]{1,0:T(4,128)}, u32[]{:S(2)}) copy-start(f32[4,16]{1,0:T(4,128)} %param.27) | copy-start | bytes 772
  162.6 8.0 %copy-start.9 = (s32[1,4]{1,0:T(1,128)S(1)}, s32[1,4]{1,0:T(1,128)}, u32[]{:S(2)}) copy-start(s32[1,4]{1,0:T(1,128)} %param.26) | copy-start | bytes 52
  213.4 3.0 copy-start.4
  213.5 4.5 copy-start.6
  357.2 0.7 copy-start.2
  362.1 0.6 copy-start.5
  369.8 2.4 copy-start.3
  374.8 0.7 copy-start.2
  379.6 0.6 copy-start.5
  387.4 2.4 copy-start.3
  544.0 8.0 %copy-start.8 = (bf16[128,4,128]{2,0,1:T(8,128)(2,1)S(1)}, bf16[128,4,128]{2,0,1:T(8,128)(2,1)}, u32[]{:S(2)}) copy-start(bf16[128,4,128]{2,0,1:T(8,128)(2,1)} %copy.90) | copy-start | bytes 393220
  599.0 1.3 copy-start.1
Sparse Core Ops, SparseCore 0:
  11.6 71.5 all-gather.4
  86.9 69.3 all-gather.6
  159.9 69.3 all-gather.10
  232.2 88.6 all-gather.8
